TPU v7x, 32 devices: a whole 2x2x4 slice. The times are simulated.
32 devices in a mesh: expert: 8 (over z, x), dp: 4 (over y, core).
Axes of the slice: x: 2, y: 2, z: 4, core: 2. Of those that a mesh axis runs over, the one named last changes fastest.
Arguments:
- tokens: bfloat16 [8, 240, 7168], P('expert', 'dp'), may hold values from -6 to 6
- cotangent: bfloat16 [8, 240, 7168], P('expert', 'dp'), may hold values from -1.5 to 1.5
- counts: int32 [8, 4], replicated, may hold values from 1 to 60, as said below
- w_gate: bfloat16 [8, 7168, 2048], P('expert', None, 'dp'), may hold values from -0.0625 to 0.0625
- w_up: bfloat16 [8, 7168, 2048], P('expert', None, 'dp'), may hold values from -0.0625 to 0.0625
- w_down: bfloat16 [8, 2048, 7168], P('expert', 'dp'), may hold values from -0.125 to 0.125
Outputs:
- outputs: bfloat16 [8, 240, 7168], P('expert', 'dp')
- input_grads: bfloat16 [8, 240, 7168], P('expert', 'dp')
- gate_grad: bfloat16 [8, 7168, 2048], P('expert', None, 'dp')
- up_grad: bfloat16 [8, 7168, 2048], P('expert', None, 'dp')
- down_grad: bfloat16 [8, 2048, 7168], P('expert', 'dp')
Inputs may be any that keep to these rules, and one draw needn't show every extreme that they name: For each expert e below 4, exactly one of experts e and e + 4 is hot: all its counts exceed 40 - 20 and one equals 60; every count of the other is at most 20 and one equals 20.
All inputs are finite; a program needn't handle non-finite values.
Results may differ from a plain program's by a relative error of at most 0.012.
Values may be sent and summed in bfloat16 or wider, within the bound.
A program may use at most 192 MiB of HBM per device.

v0:
```python
import jax
import jax.numpy as jnp
from jax import lax
from jax.sharding import PartitionSpec as P

HOME = 40
SPILL = 20


def swapped(x, axis, distance):
    return lax.ppermute(x, axis, [(i, i ^ 1 << distance) for i in range(lax.axis_size(axis))])


def silu_slope(value):
    sigma = jax.nn.sigmoid(value)
    return sigma * (1.0 + value * (1.0 - sigma))


def contract_last(left, right):
    return lax.dot_general(
        left, right, (((1,), (1,)), ((), ())), preferred_element_type=jnp.float32
    )


def contract_first(left, right):
    return lax.dot_general(
        left, right, (((0,), (0,)), ((), ())), preferred_element_type=jnp.float32
    )


def expert_work(rows, cot_rows, gate_w, up_w, down_w):
    gate = jnp.dot(rows, gate_w, preferred_element_type=jnp.float32)
    up = jnp.dot(rows, up_w, preferred_element_type=jnp.float32)
    active = jax.nn.silu(gate)
    hidden = (active * up).astype(jnp.bfloat16)
    out_part = jnp.dot(hidden, down_w, preferred_element_type=jnp.float32)
    hidden_grad = contract_last(cot_rows, down_w)
    gate_act = (hidden_grad * up * silu_slope(gate)).astype(jnp.bfloat16)
    up_act = (hidden_grad * active).astype(jnp.bfloat16)
    in_part = contract_last(gate_act, gate_w) + contract_last(up_act, up_w)
    gate_term = contract_first(rows, gate_act)
    up_term = contract_first(rows, up_act)
    down_term = contract_first(hidden, cot_rows)
    return (out_part, in_part, gate_term, up_term, down_term)


def shards(tokens, cotangent, counts, w_gate, w_up, w_down):
    rows_in = tokens[0]
    cot_in = cotangent[0]
    gate_w = w_gate[0]
    up_w = w_up[0]
    down_w = w_down[0]
    expert_total = lax.axis_size("expert")
    expert_pos = lax.axis_index("expert")
    batch_pos = lax.axis_index("dp")
    expert_ids = jnp.arange(counts.shape[0], dtype=jnp.int32)
    batch_ids = jnp.arange(counts.shape[1], dtype=jnp.int32)
    own_counts = jnp.sum(jnp.where(expert_ids[:, None] == expert_pos, counts, 0), axis=0)
    own_total = jnp.sum(jnp.where(batch_ids == batch_pos, own_counts, 0))
    own_hot = jnp.max(own_counts) > HOME - SPILL
    slots = rows_in.shape[0]
    valid = (jnp.arange(slots, dtype=jnp.int32) < own_total)[:, None]
    masked = jnp.where(valid, rows_in, jnp.zeros_like(rows_in))
    masked_cot = jnp.where(valid, cot_in, jnp.zeros_like(cot_in))
    partner_bit = expert_total.bit_length() - 2
    border = HOME - SPILL
    got_rows, got_cot, far_gate, far_up, far_down = swapped(
        (masked[HOME:], masked_cot[HOME:], gate_w, up_w, down_w), "expert", partner_bit
    )
    region_rows = masked[border:HOME] + got_rows
    region_cot = masked_cot[border:HOME] + got_cot
    pick_gate = jnp.where(own_hot, gate_w, far_gate)
    pick_up = jnp.where(own_hot, up_w, far_up)
    pick_down = jnp.where(own_hot, down_w, far_down)
    all_home, all_region, cot_home, cot_region = (
        lax.all_gather(masked[:border], "dp", axis=0, tiled=True),
        lax.all_gather(region_rows, "dp", axis=0, tiled=True),
        lax.all_gather(masked_cot[:border], "dp", axis=0, tiled=True),
        lax.all_gather(region_cot, "dp", axis=0, tiled=True),
    )
    home_res = expert_work(all_home, cot_home, gate_w, up_w, down_w)
    region_res = expert_work(all_region, cot_region, pick_gate, pick_up, pick_down)
    home_out, region_sum_out, home_in, region_sum_in = (
        lax.psum_scatter(
            home_res[0].astype(jnp.bfloat16), "dp", scatter_dimension=0, tiled=True
        ).astype(jnp.float32),
        lax.psum_scatter(
            region_res[0].astype(jnp.bfloat16), "dp", scatter_dimension=0, tiled=True
        ).astype(jnp.float32),
        lax.psum_scatter(
            home_res[1].astype(jnp.bfloat16), "dp", scatter_dimension=0, tiled=True
        ).astype(jnp.float32),
        lax.psum_scatter(
            region_res[1].astype(jnp.bfloat16), "dp", scatter_dimension=0, tiled=True
        ).astype(jnp.float32),
    )
    region_out = region_sum_out.astype(jnp.bfloat16)
    region_in = region_sum_in.astype(jnp.bfloat16)
    blank = jnp.zeros_like(region_out)
    back_out, back_in = swapped(
        (jnp.where(own_hot, blank, region_out), jnp.where(own_hot, blank, region_in)),
        "expert",
        partner_bit,
    )
    outputs = jnp.concatenate(
        [home_out.astype(jnp.bfloat16), jnp.where(own_hot, region_out, blank), back_out], axis=0
    )
    input_grads = jnp.concatenate(
        [home_in.astype(jnp.bfloat16), jnp.where(own_hot, region_in, blank), back_in], axis=0
    )
    kept = [home_res[k] + jnp.where(own_hot, region_res[k], 0.0) for k in (2, 3, 4)]
    sending = [jnp.where(own_hot, 0.0, region_res[k]).astype(jnp.bfloat16) for k in (2, 3, 4)]
    got_gate, got_up, got_down = swapped(
        (sending[0], sending[1], sending[2]), "expert", partner_bit
    )
    gate_grad = (kept[0] + got_gate.astype(jnp.float32)).astype(jnp.bfloat16)
    up_grad = (kept[1] + got_up.astype(jnp.float32)).astype(jnp.bfloat16)
    down_grad = (kept[2] + got_down.astype(jnp.float32)).astype(jnp.bfloat16)
    return (outputs[None], input_grads[None], gate_grad[None], up_grad[None], down_grad[None])


def solution(mesh):
    placed = (
        P("expert", "dp", None),
        P("expert", "dp", None),
        P(),
        P("expert", None, "dp"),
        P("expert", None, "dp"),
        P("expert", "dp", None),
    )
    return jax.shard_map(
        shards,
        mesh=mesh,
        in_specs=placed,
        out_specs=(
            P("expert", "dp", None),
            P("expert", "dp", None),
            P("expert", None, "dp"),
            P("expert", None, "dp"),
            P("expert", "dp", None),
        ),
        check_vma=False,
    )
```

profile of v0, /device:TPU:0, one launch (start us, length us, event | category | flops | bytes accessed | tf_op | source)
XLA Modules:
  0.0 2024.2 jit_solution(11692155397770165445)
XLA Ops:
  7.2 0.8 select_reduce_fusion
  8.0 0.6 fusion.17
  8.7 0.6 iota_compare_fusion.1
  9.3 1.6 bitcast_select_fusion
  11.0 0.8 slice_bitcast_fusion
  11.8 4.1 collective-permute-start.5
  16.0 0.8 slice_bitcast_fusion.1
  16.9 2.9 collective-permute-start
  19.9 2.8 collective-permute-start.1
  22.7 488.8 %collective-permute-done.5 = bf16[20,7168]{1,0:T(8,128)(2,1)S(1)} collective-permute-done((bf16[20,7168]{1,0:T(8,128)(2,1)S(1)}, bf16[20,7168]{1,0:T(8,128)(2,1)S(1)}, u32[]{:S(2)}, u32[]{:S(2)}) %collective-permute-start.5) | collective-permute-done | bytes 286752 | tf_op jit(solution)/shard_map/ppermute | solution.py:11
  511.5 0.8 fusion.13
  513.0 163.1 %collective-permute-done = bf16[20,7168]{1,0:T(8,128)(2,1)S(1)} collective-permute-done((bf16[20,7168]{1,0:T(8,128)(2,1)S(1)}, bf16[20,7168]{1,0:T(8,128)(2,1)S(1)}, u32[]{:S(2)}, u32[]{:S(2)}) %collective-permute-start) | collective-permute-done | bytes 286752 | tf_op jit(solution)/shard_map/ppermute | solution.py:11
  676.1 0.8 fusion.14
  677.0 2.3 reshape.24
  679.3 2.5 reshape.20
  681.8 5.2 fusion.26
  687.2 1.4 fusion.32
  688.6 1.0 slice-done.9
  689.6 0.2 copy-done.3
  689.8 2.4 multiply_convert_fusion.2
  692.2 2.5 convolution_convert_fusion.1
  694.7 2.3 fusion.29
  697.0 0.8 slice-done.1
  697.8 3.4 fusion.7
  701.3 2.3 reshape.26
  703.6 2.4 reshape.22
  706.0 5.9 fusion.12
  711.9 121.6 %collective-permute-done.2 = bf16[7168,512]{1,0:T(8,128)(2,1)} collective-permute-done((bf16[7168,512]{1,0:T(8,128)(2,1)}, bf16[7168,512]{1,0:T(8,128)(2,1)}, u32[]{:S(2)}, u32[]{:S(2)}) %collective-permute-start.2) | collective-permute-done | bytes 7340064 | tf_op jit(solution)/shard_map/ppermute | solution.py:11
  833.5 1.3 fusion.11
  834.9 155.1 %collective-permute-done.1 = bf16[7168,512]{1,0:T(8,128)(2,1)} collective-permute-done((bf16[7168,512]{1,0:T(8,128)(2,1)}, bf16[7168,512]{1,0:T(8,128)(2,1)}, u32[]{:S(2)}, u32[]{:S(2)}) %collective-permute-start.1) | collective-permute-done | bytes 7340064 | tf_op jit(solution)/shard_map/ppermute | solution.py:11
  990.0 4.5 multiply_convert_fusion.1
  994.5 10.0 select_convert_fusion
  1004.5 1.6 collective-permute-start.9
  1006.1 10.0 select_convert_fusion.1
  1016.1 1.3 collective-permute-start.8
  1017.4 10.0 select_convert_fusion.2
  1027.4 1.6 collective-permute-start.7
  1029.0 2.6 convolution_convert_fusion
  1031.6 2.6 fusion.10
  1034.2 2.5 fusion.8
  1036.8 50.9 %fusion.34 = (bf16[24,7168]{1,0:T(8,128)(2,1)}, bf16[24,7168]{1,0:T(8,128)(2,1)}, bf16[24,7168]{1,0:T(8,128)(2,1)}, bf16[24,7168]{1,0:T(8,128)(2,1)}) fusion(bf16[80,7168]{1,0:T(8,128)(2,1)} %convolution_convert_fusion, bf16[80,7168]{1,0:T(8,128)(2,1)S(1)} %copy-done.6, bf16[80,7168]{1,0:T(8,128)(2,1)S(1)} %fusion.8, bf16[80,7168]{1,0:T(8,128)(2,1)S(1)} %copy-done.7), kind=kCustom, calls=%all-reduce-scatter.4 | all-reduce-scatter fusion | flops 2752513 | bytes 5964288
  1087.7 1.1 slice.31
  1088.8 1.3 collective-permute-start.11
  1090.1 1.0 slice.32
  1091.1 3.4 collective-permute-start.12
  1094.6 0.7 dynamic-slice.10
  1096.0 1.0 slice.30
  1097.0 1.0 slice.33
  1098.0 2.6 collective-permute-start.13
  1100.6 3.6 concatenate.9
  1104.2 0.7 copy-done.12
  1104.9 2.0 collective-permute-start.10
  1106.9 0.9 broadcast_select_fusion.12
  1107.7 4.5 concatenate.10
  1112.2 11.1 collective-permute-start.4
  1123.3 4.5 concatenate.11
  1127.8 4.5 concatenate.8
  1132.7 842.5 %collective-permute-done.4 = bf16[20,7168]{1,0:T(8,128)(2,1)} collective-permute-done((bf16[20,7168]{1,0:T(8,128)(2,1)}, bf16[20,7168]{1,0:T(8,128)(2,1)}, u32[]{:S(2)}, u32[]{:S(2)}) %collective-permute-start.4) | collective-permute-done | bytes 286752 | tf_op jit(solution)/shard_map/ppermute | solution.py:11
  1975.2 2.1 maximum_bitcast_fusion
  1977.3 3.5 collective-permute-done.6
  1980.7 1.1 maximum_bitcast_fusion.1
  1981.9 12.0 fusion.6
  1993.9 11.9 fusion.5
  2005.8 11.9 fusion.4
  (81 shorter events, 1.2 us)
Async XLA Ops:
  7.2 669.8 %all-gather.13.cloned.1.call-start = ((), (), s32[]{:S(2)}) async-start(), calls=%async_computation.2 | async-start | bytes 1720320 | tf_op jit(solution)/shard_map/all_gather | solution.py:78
  11.8 667.5 %all-gather.9.cloned.1.call-start = ((), (), s32[]{:S(2)}) async-start(), calls=%async_computation | async-start | bytes 1720320 | tf_op jit(solution)/shard_map/all_gather | solution.py:76
  11.8 499.6 %collective-permute-start.5 = (bf16[20,7168]{1,0:T(8,128)(2,1)S(1)}, bf16[20,7168]{1,0:T(8,128)(2,1)S(1)}, u32[]{:S(2)}, u32[]{:S(2)}) collective-permute-start(bf16[20,7168]{1,0:T(8,128)(2,1)S(1)} %get-tuple-element.16), channel_id=1, source_target_pairs={{0,16},{4,20},{8,24},{12,28},{16,0},{20,4},{24,8},{28,12},{1,17},{... | collective-permute-start | bytes 860168 | tf_op jit(solution)/shard_map/ppermute | solution.py:11
  15.9 690.0 %collective-permute-start.3 = (bf16[512,7168]{1,0:T(8,128)(2,1)}, bf16[512,7168]{1,0:T(8,128)(2,1)}, u32[]{:S(2)}, u32[]{:S(2)}) collective-permute-start(bf16[512,7168]{1,0:T(8,128)(2,1)} %bitcast.109), channel_id=1, source_target_pairs={{0,16},{4,20},{8,24},{12,28},{16,0},{20,4},{24,8},{28,12},{1,17},{... | collective-permute-start | bytes 22020104 | tf_op jit(solution)/shard_map/ppermute | solution.py:11
  16.8 684.5 %all-gather.15.cloned.1.call-start = ((), (), s32[]{:S(2)}) async-start(), calls=%async_computation.3 | async-start | bytes 1720320 | tf_op jit(solution)/shard_map/all_gather | solution.py:79
  16.9 659.2 %collective-permute-start = (bf16[20,7168]{1,0:T(8,128)(2,1)S(1)}, bf16[20,7168]{1,0:T(8,128)(2,1)S(1)}, u32[]{:S(2)}, u32[]{:S(2)}) collective-permute-start(bf16[20,7168]{1,0:T(8,128)(2,1)S(1)} %get-tuple-element.18), channel_id=1, source_target_pairs={{0,16},{4,20},{8,24},{12,28},{16,0},{20,4},{24,8},{28,12},{1,17},{... | collective-permute-start | bytes 860168 | tf_op jit(solution)/shard_map/ppermute | solution.py:11
  19.8 813.8 %collective-permute-start.2 = (bf16[7168,512]{1,0:T(8,128)(2,1)}, bf16[7168,512]{1,0:T(8,128)(2,1)}, u32[]{:S(2)}, u32[]{:S(2)}) collective-permute-start(bf16[7168,512]{1,0:T(8,128)(2,1)} %bitcast.99), channel_id=1, source_target_pairs={{0,16},{4,20},{8,24},{12,28},{16,0},{20,4},{24,8},{28,12},{1,17},{... | collective-permute-start | bytes 22020104 | tf_op jit(solution)/shard_map/ppermute | solution.py:11
  19.9 970.1 %collective-permute-start.1 = (bf16[7168,512]{1,0:T(8,128)(2,1)}, bf16[7168,512]{1,0:T(8,128)(2,1)}, u32[]{:S(2)}, u32[]{:S(2)}) collective-permute-start(bf16[7168,512]{1,0:T(8,128)(2,1)} %bitcast.104), channel_id=1, source_target_pairs={{0,16},{4,20},{8,24},{12,28},{16,0},{20,4},{24,8},{28,12},{1,17},{... | collective-permute-start | bytes 22020104 | tf_op jit(solution)/shard_map/ppermute | solution.py:11
  512.3 191.2 %all-gather.11.cloned.1.call-start = ((), (), s32[]{:S(2)}) async-start(), calls=%async_computation.1 | async-start | bytes 1720320 | tf_op jit(solution)/shard_map/all_gather | solution.py:77
  679.3 7.7 slice-start.4
  681.8 5.3 slice-start.5
  681.8 5.4 copy-start
  681.8 6.8 slice-start.8
  687.2 2.4 slice-start.9
  687.2 2.6 copy-start.3
  692.2 4.8 copy-start.8
  692.2 4.8 copy-start.10
  694.7 2.3 slice-start
  694.7 3.2 slice-start.1
  703.6 130.0 %slice-start.2 = ((s8[7340032]{0:T(1024)(128)(4,1)}), s8[3145728]{0:T(1024)(128)(4,1)S(1)}, s32[]{:S(2)}) async-start(s8[7340032]{0:T(1024)(128)(4,1)} %bitcast.102), calls=%async_computation.6 | async-start | bytes 6291456
  706.0 127.6 %slice-start.3 = ((s8[7340032]{0:T(1024)(128)(4,1)}), s8[4194304]{0:T(1024)(128)(4,1)S(1)}, s32[]{:S(2)}) async-start(s8[7340032]{0:T(1024)(128)(4,1)} %bitcast.102), calls=%async_computation.7 | async-start | bytes 8388608
  706.0 127.6 %copy-start.2 = (bf16[80,7168]{1,0:T(8,128)(2,1)S(1)}, bf16[80,7168]{1,0:T(8,128)(2,1)}, u32[]{:S(2)}) copy-start(bf16[80,7168]{1,0:T(8,128)(2,1)} %reshape.22) | copy-start | bytes 3440644
  834.9 159.6 %copy-start.5 = (bf16[80,7168]{1,0:T(8,128)(2,1)S(1)}, bf16[80,7168]{1,0:T(8,128)(2,1)}, u32[]{:S(2)}) copy-start(bf16[80,7168]{1,0:T(8,128)(2,1)} %reshape.26) | copy-start | bytes 3440644
  1004.5 977.3 %collective-permute-start.9 = (bf16[512,7168]{1,0:T(8,128)(2,1)}, bf16[512,7168]{1,0:T(8,128)(2,1)}, u32[]{:S(2)}, u32[]{:S(2)}) collective-permute-start(bf16[512,7168]{1,0:T(8,128)(2,1)} %get-tuple-element.35), channel_id=1, source_target_pairs={{0,16},{4,20},{8,24},{12,28},{16,0},{20,4},{24,8},{28,12},{1,17},{... | collective-permute-start | bytes 22020104 | tf_op jit(solution)/shard_map/ppermute | solution.py:11
  1006.1 22.9 %slice-start.10 = ((s8[7340032]{0:T(1024)(128)(4,1)}), s8[4194304]{0:T(1024)(128)(4,1)S(1)}, s32[]{:S(2)}) async-start(s8[7340032]{0:T(1024)(128)(4,1)} %bitcast.112), calls=%async_computation.14 | async-start | bytes 8388608
  1016.1 12.9 slice-start.11
  1016.1 977.7 %collective-permute-start.8 = (bf16[7168,512]{1,0:T(8,128)(2,1)}, bf16[7168,512]{1,0:T(8,128)(2,1)}, u32[]{:S(2)}, u32[]{:S(2)}) collective-permute-start(bf16[7168,512]{1,0:T(8,128)(2,1)} %get-tuple-element.33), channel_id=1, source_target_pairs={{0,16},{4,20},{8,24},{12,28},{16,0},{20,4},{24,8},{28,12},{1,17},{... | collective-permute-start | bytes 22020104 | tf_op jit(solution)/shard_map/ppermute | solution.py:11
  1027.4 978.4 %collective-permute-start.7 = (bf16[7168,512]{1,0:T(8,128)(2,1)}, bf16[7168,512]{1,0:T(8,128)(2,1)}, u32[]{:S(2)}, u32[]{:S(2)}) collective-permute-start(bf16[7168,512]{1,0:T(8,128)(2,1)} %get-tuple-element.31), channel_id=1, source_target_pairs={{0,16},{4,20},{8,24},{12,28},{16,0},{20,4},{24,8},{28,12},{1,17},{... | collective-permute-start | bytes 22020104 | tf_op jit(solution)/shard_map/ppermute | solution.py:11
  1029.0 5.2 slice-start.6
  1031.6 2.6 slice-start.7
  1034.2 2.6 copy-start.6
  1034.2 2.6 copy-start.7
  1034.2 60.4 %copy-start.13 = (u32[32]{0:T(128)S(1)}, u32[32]{0:T(128)}, u32[]{:S(2)}) copy-start(u32[32]{0:T(128)} %constant.32) | copy-start | bytes 388
  1087.7 894.1 %copy-start.4 = (bf16[80,7168]{1,0:T(8,128)(2,1)S(1)}, bf16[80,7168]{1,0:T(8,128)(2,1)}, u32[]{:S(2)}) copy-start(bf16[80,7168]{1,0:T(8,128)(2,1)} %reshape.24) | copy-start | bytes 3440644
  1087.7 894.1 %copy-start.9 = (bf16[80,512]{1,0:T(8,128)(2,1)S(1)}, bf16[80,512]{1,0:T(8,128)(2,1)}, u32[]{:S(2)}) copy-start(bf16[80,512]{1,0:T(8,128)(2,1)} %copy-done.8) | copy-start | bytes 245764
  1088.8 9.1 collective-permute-start.11
  1091.1 13.1 collective-permute-start.12
  1098.0 14.2 collective-permute-start.13
  1104.2 0.7 copy-start.12
  1104.9 22.9 %collective-permute-start.10 = (bf16[12,7168]{1,0:T(8,128)(2,1)S(1)}, bf16[12,7168]{1,0:T(8,128)(2,1)}, u32[]{:S(2)}, u32[]{:S(2)}) collective-permute-start(bf16[12,7168]{1,0:T(8,128)(2,1)S(1)} %slice.30), channel_id=1, source_target_pairs={{0,1},{1,2},{2,3},{4,5},{5,6},{6,7},{8,9},{9,10},{10,11},{12,13},{... | collective-permute-start | bytes 516104
  1112.2 863.0 %collective-permute-start.4 = (bf16[20,7168]{1,0:T(8,128)(2,1)}, bf16[20,7168]{1,0:T(8,128)(2,1)}, u32[]{:S(2)}, u32[]{:S(2)}) collective-permute-start(bf16[20,7168]{1,0:T(8,128)(2,1)} %get-tuple-element.22), channel_id=1, source_target_pairs={{0,16},{4,20},{8,24},{12,28},{16,0},{20,4},{24,8},{28,12},{1,17},{... | collective-permute-start | bytes 860168 | tf_op jit(solution)/shard_map/ppermute | solution.py:11
  1132.6 848.1 %collective-permute-start.6 = (bf16[20,7168]{1,0:T(8,128)(2,1)S(1)}, bf16[20,7168]{1,0:T(8,128)(2,1)S(1)}, u32[]{:S(2)}, u32[]{:S(2)}) collective-permute-start(bf16[20,7168]{1,0:T(8,128)(2,1)S(1)} %get-tuple-element.20), channel_id=1, source_target_pairs={{0,16},{4,20},{8,24},{12,28},{16,0},{20,4},{24,8},{28,12},{1,17},{... | collective-permute-start | bytes 860168 | tf_op jit(solution)/shard_map/ppermute | solution.py:11
  1981.8 12.0 copy-start.1
  1981.8 12.0 copy-start.11
Sparse Core Ops, SparseCore 0:
  11.9 21.2 all-gather.12
  35.3 18.5 all-gather.8
  512.4 19.0 all-gather.14
  677.1 19.0 all-gather.10
where the time goes:
time: 2030 us; the launch traced here: 2020 us
  waiting for transfers between devices  1770 us (87%)
  matrix products  102 us (5%)
  blocking collectives  50.9 us (3%)
  local copies, waits for them, and re-layouts  35.9 us (2%)
  starting transfers between devices  35.2 us (2%)
    ppermute x10, waiting for transfers between devices, swapped(): lax.ppermute(x, axis, [(i, i ^ 1 << distance) for i in range(lax.axis_siz...  1770 us
    dot_general x6, matrix products, contract_first(): lax.dot_general(left, right, (((0,), (0,)), ((), ())), preferred_element_...  65.7 us
    unnamed x1, blocking collectives  50.9 us
  transfers between devices with their start and end apart: 18, of which 6 were waited for; matrix products, arithmetic and copies ran while one was open for 8% of the time, Pallas kernels for 0%

commit v1 on v0

v1 whole, which is shorter than its diff:
```python
import jax
import jax.numpy as jnp
from jax import lax
from jax.sharding import PartitionSpec as P


def silu_slope(value):
    sigma = jax.nn.sigmoid(value)
    return sigma * (1.0 + value * (1.0 - sigma))


def contract_last(left, right):
    return lax.dot_general(
        left, right, (((1,), (1,)), ((), ())), preferred_element_type=jnp.float32
    )


def contract_first(left, right):
    return lax.dot_general(
        left, right, (((0,), (0,)), ((), ())), preferred_element_type=jnp.float32
    )


def shards(tokens, cotangent, counts, w_gate, w_up, w_down):
    gate_w = w_gate[0]
    up_w = w_up[0]
    down_w = w_down[0]
    own_total = counts[lax.axis_index("expert"), lax.axis_index("dp")]
    slots = tokens.shape[1]
    valid = (jnp.arange(slots, dtype=jnp.int32) < own_total)[:, None]
    both = jnp.stack([jnp.where(valid, tokens[0], 0), jnp.where(valid, cotangent[0], 0)])
    full = lax.all_gather(both, "dp", axis=1, tiled=True)
    rows, cot_rows = full[0], full[1]
    gate = jnp.dot(rows, gate_w, preferred_element_type=jnp.float32)
    up = jnp.dot(rows, up_w, preferred_element_type=jnp.float32)
    active = jax.nn.silu(gate)
    hidden = (active * up).astype(jnp.bfloat16)
    hidden_grad = contract_last(cot_rows, down_w)
    gate_act = (hidden_grad * up * silu_slope(gate)).astype(jnp.bfloat16)
    up_act = (hidden_grad * active).astype(jnp.bfloat16)
    out_part = jnp.dot(hidden, down_w, preferred_element_type=jnp.float32)
    in_part = contract_last(gate_act, gate_w) + contract_last(up_act, up_w)
    parts = jnp.stack([out_part.astype(jnp.bfloat16), in_part.astype(jnp.bfloat16)])
    sums = lax.psum_scatter(parts, "dp", scatter_dimension=1, tiled=True)
    gate_grad = contract_first(rows, gate_act).astype(jnp.bfloat16)
    up_grad = contract_first(rows, up_act).astype(jnp.bfloat16)
    down_grad = contract_first(hidden, cot_rows).astype(jnp.bfloat16)
    return (sums[0][None], sums[1][None], gate_grad[None], up_grad[None], down_grad[None])


def solution(mesh):
    by_row = P("expert", "dp", None)
    by_column = P("expert", None, "dp")
    return jax.shard_map(
        shards,
        mesh=mesh,
        in_specs=(by_row, by_row, P(), by_column, by_column, by_row),
        out_specs=(by_row, by_row, by_column, by_column, by_row),
        check_vma=False,
    )
```

time: 2030 us -> 298 us (0.15)
  waiting for transfers between devices: 1770 us -> 161 us
  matrix products: 102 us -> 51.1 us
  blocking collectives: 50.9 us -> 0 us
  starting transfers between devices: 35.2 us -> 0.08 us
  local copies, waits for them, and re-layouts: 35.9 us -> 56.7 us
    ppermute x10 -> x0, waiting for transfers between devices: 1770 us -> none  [swapped(): lax.ppermute(x, axis, [(i, i ^ 1 << distance) for i in range(lax.axis_siz...]
    unnamed x8 -> x3, waiting for transfers between devices: 0.08 us -> 108 us
    all_gather x4 -> x1, waiting for transfers between devices: 0.03 us -> 52.5 us  [shards(): full = lax.all_gather(both, 'dp', axis=1, tiled=True)]
    unnamed x1 -> x0, blocking collectives: 50.9 us -> none
    dot_general x6 -> x3, matrix products: 65.7 us -> 19 us  [contract_first(): lax.dot_general(left, right, (((0,), (0,)), ((), ())), preferred_element_...]
    another operation x0 -> x1, local copies, waits for them, and re-layouts: none -> 32.2 us  [shards(): jnp.stack([out_part.astype(jnp.bfloat16), in_part.astype(jnp.bfloat16)])]
    unnamed x69 -> x22, local copies, waits for them, and re-layouts: 35.9 us -> 4.72 us
    ppermute x10 -> x0, starting transfers between devices: 25.7 us -> none  [swapped(): lax.ppermute(x, axis, [(i, i ^ 1 << distance) for i in range(lax.axis_siz...]
  transfers between devices with their start and end apart: 18 -> 2, of which waited for: 6 -> 2; matrix products, arithmetic and copies ran while one was open for 8% -> 7% of each run, Pallas kernels for 0% -> 0%
where the time goes in v1:
time: 298 us; the launch traced here: 297 us
  waiting for transfers between devices  161 us (54%)
  local copies, waits for them, and re-layouts  56.7 us (19%)
  matrix products  51.1 us (17%)
  between operations  14.9 us (5%)
  other arithmetic  13.5 us (5%)
    unnamed x3, waiting for transfers between devices  108 us
    all_gather x1, waiting for transfers between devices, shards(): full = lax.all_gather(both, 'dp', axis=1, tiled=True)  52.5 us
    another operation x1, local copies, waits for them, and re-layouts, shards(): jnp.stack([out_part.astype(jnp.bfloat16), in_part.astype(jnp.bfloat16)])  32.2 us
    dot_general x3, matrix products, contract_first(): lax.dot_general(left, right, (((0,), (0,)), ((), ())), preferred_element_...  19 us
    dot_general x3, matrix products, contract_last(): lax.dot_general(left, right, (((1,), (1,)), ((), ())), preferred_element_...  17.3 us
    slice x1, local copies, waits for them, and re-layouts, shards(): rows, cot_rows = (full[0], full[1])  13.7 us
    dot_general x1, matrix products, shards(): gate = jnp.dot(rows, gate_w, preferred_element_type=jnp.float32)  7.37 us
  transfers between devices with their start and end apart: 2, of which 2 were waited for; matrix products, arithmetic and copies ran while one was open for 7% of the time, Pallas kernels for 0%

profile of v1, /device:TPU:0, one launch (start us, length us, event | category | flops | bytes accessed | tf_op | source)
XLA Modules:
  0.0 297.3 jit_solution(3302341033518518923)
XLA Ops:
  7.2 0.0 all-gather.2.cloned.1.call-start
  7.2 1.3 dynamic_slice.3
  8.5 0.6 iota_compare_fusion
  9.1 5.2 %broadcast_select_fusion.1 = (bf16[1,60,7168]{2,0,1:T(2,128)(2,1)S(1)}, bf16[1,60,7168]{2,0,1:T(2,128)(2,1)S(1)}) fusion(pred[60]{0:T(512)(128)(4,1)S(1)} %iota_compare_fusion, bf16[1,60,7168]{2,1,0:T(8,128)(2,1)} %param.6, bf16[1,60,7168]{2,1,0:T(8,128)(2,1)} %param.7), kind=kLoop, calls=%fused_computation.25 | loop fusion | flops 860160 | bytes 3440700 | tf_op jit(solution)/shard_map/jit(_where)/select_n | solution.py:31
  14.3 5.1 %pad_maximum_fusion.1 = bf16[2,60,7168]{2,0,1:T(2,128)(2,1)} fusion(bf16[1,60,7168]{2,0,1:T(2,128)(2,1)S(1)} %get-tuple-element.23, bf16[1,60,7168]{2,0,1:T(2,128)(2,1)S(1)} %get-tuple-element.22), kind=kLoop, calls=%fused_computation.26 | loop fusion | flops 3440640 | bytes 3440640 | tf_op jit(solution)/shard_map/stack | solution.py:31
  19.4 0.0 all-gather.2.cloned.1.call-update
  19.4 0.0 all-reduce.3.cloned.1.call-start
  19.5 52.5 %all-gather.2.cloned.1.call-done = bf16[2,240,7168]{2,0,1:T(2,128)(2,1)} async-done(((bf16[2,60,7168]{2,0,1:T(2,128)(2,1)}), bf16[2,240,7168]{2,0,1:T(2,128)(2,1)}) %all-gather.2.cloned.1.call-update) | async-done | bytes 6881296 | tf_op jit(solution)/shard_map/all_gather | solution.py:32
  72.0 13.7 %fusion.17 = (bf16[1,240,7168]{2,0,1:T(2,128)(2,1)S(1)}, bf16[1,240,7168]{2,0,1:T(2,128)(2,1)S(1)}) fusion(bf16[2,240,7168]{2,0,1:T(2,128)(2,1)} %all-gather.2.cloned.1.call-done), kind=kLoop, calls=%fused_computation.35 | loop fusion | bytes 13762560 | tf_op jit(solution)/shard_map/slice | solution.py:33
  85.7 0.0 copy-start
  85.7 0.0 slice-start
  85.8 1.1 copy.31
  86.8 0.0 slice-start.1
  86.8 7.4 %fusion.14 = f32[240,512]{1,0:T(8,128)S(1)} fusion(bf16[240,7168]{1,0:T(8,128)(2,1)S(1)} %bitcast.46, bf16[1,7168,512]{2,1,0:T(8,128)(2,1)} %param.9), kind=kOutput, calls=%fused_computation.19 | convolution fusion | flops 1761607680 | bytes 11272192 | tf_op jit(solution)/shard_map/dot_general | solution.py:34
  94.2 0.0 copy-done
  94.2 5.2 %fusion.6 = f32[240,512]{1,0:T(8,128)S(1)} fusion(bf16[1,512,7168]{2,1,0:T(8,128)(2,1)} %param.11, bf16[1,240,7168]{2,0,1:T(2,128)(2,1)S(1)} %get-tuple-element.17), kind=kOutput, calls=%fused_computation.11 | convolution fusion | flops 1761607680 | bytes 11272192 | tf_op jit(solution)/shard_map/dot_general | solution.py:13
  99.4 0.0 slice-done
  99.4 0.0 slice-done.1
  99.4 2.2 multiply_convert_fusion.2
  101.6 0.0 copy-start.3
  101.6 0.0 copy-start.4
  101.6 0.0 copy-start.1
  101.6 5.3 %fusion.4 = bf16[1,240,7168]{2,1,0:T(8,128)(2,1)S(1)} fusion(bf16[240,512]{1,0:T(8,128)(2,1)S(1)} %get-tuple-element.19, bf16[1,512,7168]{2,1,0:T(8,128)(2,1)} %param.11), kind=kOutput, calls=%fused_computation.9 | convolution fusion | flops 1763328000 | bytes 11026432 | tf_op jit(solution)/shard_map/dot_general | solution.py:41
  106.9 5.2 %fusion.12 = f32[240,7168]{1,0:T(8,128)S(1)} fusion(bf16[240,512]{1,0:T(8,128)(2,1)S(1)} %get-tuple-element.20, bf16[1,7168,512]{2,1,0:T(8,128)(2,1)} %param.9), kind=kOutput, calls=%fused_computation.17 | convolution fusion | flops 1761607680 | bytes 14467072 | tf_op jit(solution)/shard_map/dot_general | solution.py:13
  112.1 0.0 copy-done.3
  112.1 0.0 copy-done.4
  112.1 0.0 copy-done.1
  112.2 7.0 %fusion.5 = bf16[1,240,7168]{2,1,0:T(8,128)(2,1)} fusion(f32[240,7168]{1,0:T(8,128)S(1)} %fusion.12, bf16[240,512]{1,0:T(8,128)(2,1)S(1)} %get-tuple-element.21, bf16[1,7168,512]{2,1,0:T(8,128)(2,1)} %param.10), kind=kOutput, calls=%fused_computation.10 | convolution fusion | flops 1765048320 | bytes 17907712 | tf_op jit(solution)/shard_map/dot_general | solution.py:13
  119.1 2.6 pad_maximum_fusion
  121.7 32.2 %copy.20 = bf16[2,240,7168]{2,0,1:T(2,128)(2,1)} copy(bf16[2,240,7168]{2,1,0:T(8,128)(2,1)S(1)} %pad_maximum_fusion) | data formatting | bytes 13762560 | tf_op jit(solution)/shard_map/stack | solution.py:43
  153.9 0.0 copy-start.6
  153.9 0.0 all-reduce.3.cloned.1.call-update
  154.0 0.6 copy-done.6
  154.6 0.6 dynamic-slice
  155.8 0.0 copy-start.2
  155.8 8.6 %fusion.2 = bf16[1,512,7168]{2,1,0:T(8,128)(2,1)} fusion(bf16[240,512]{1,0:T(8,128)(2,1)} %copy-done.3, bf16[1,240,7168]{2,0,1:T(2,128)(2,1)} %copy-done), kind=kOutput, calls=%fused_computation.5 | convolution fusion | flops 1765277696 | bytes 11026432 | tf_op jit(solution)/shard_map/dot_general | solution.py:19
  164.5 0.0 copy-done.2
  164.5 0.0 copy-start.5
  164.5 5.2 %fusion.1 = bf16[1,7168,512]{2,1,0:T(8,128)(2,1)} fusion(bf16[240,7168]{1,0:T(8,128)(2,1)S(1)} %bitcast.48, bf16[240,512]{1,0:T(8,128)(2,1)S(1)} %copy-done.2), kind=kOutput, calls=%fused_computation.4 | convolution fusion | flops 1765277696 | bytes 11026432 | tf_op jit(solution)/shard_map/dot_general | solution.py:19
  169.6 0.0 copy-done.5
  169.6 5.2 %fusion = bf16[1,7168,512]{2,1,0:T(8,128)(2,1)} fusion(bf16[240,7168]{1,0:T(8,128)(2,1)S(1)} %bitcast.49, bf16[240,512]{1,0:T(8,128)(2,1)S(1)} %copy-done.5), kind=kOutput, calls=%fused_computation.3 | convolution fusion | flops 1765277696 | bytes 11026432 | tf_op jit(solution)/shard_map/dot_general | solution.py:19
  174.8 108.4 %all-reduce.3.cloned.1.call-done = bf16[2,240,7168]{2,0,1:T(2,128)(2,1)} async-done(((bf16[2,240,7168]{2,0,1:T(2,128)(2,1)}), bf16[2,240,7168]{2,0,1:T(2,128)(2,1)}) %all-reduce.3.cloned.1.call-update) | async-done | bytes 6881296
  283.3 4.8 %constant_dynamic-slice_fusion.1 = (bf16[1,60,7168]{2,0,1:T(2,128)(2,1)S(1)}, bf16[1,60,7168]{2,0,1:T(2,128)(2,1)S(1)}) fusion(bf16[2,240,7168]{2,0,1:T(2,128)(2,1)} %all-reduce.3.cloned.1.call-done, u32[]{:T(128)S(6)} %convert, u32[]{:T(128)S(6)} %multiply.1), kind=kLoop, calls=%fused_computation.33 | loop fusion | bytes 3440648 | tf_op jit(solution)/shard_map/slice | solution.py:48
  288.1 1.2 copy.22
  289.3 1.2 copy.21
  (1 shorter events, 0.0 us)
Async XLA Ops:
  7.2 64.9 %all-gather.2.cloned.1.call-start = ((), (), s32[]{:S(2)}) async-start(), calls=%async_computation | async-start | bytes 8601600 | tf_op jit(solution)/shard_map/all_gather | solution.py:32
  19.4 263.8 %all-reduce.3.cloned.1.call-start = ((), (), s32[]{:S(2)}) async-start(), calls=%async_computation.1 | async-start | bytes 13762560
  85.7 8.5 %copy-start = (bf16[1,240,7168]{2,0,1:T(2,128)(2,1)}, bf16[1,240,7168]{2,0,1:T(2,128)(2,1)S(1)}, u32[]{:S(2)}) copy-start(bf16[1,240,7168]{2,0,1:T(2,128)(2,1)S(1)} %get-tuple-element.17) | copy-start | bytes 10321924
  85.7 13.7 %slice-start = ((s8[7340032]{0:T(1024)(128)(4,1)}), s8[3145728]{0:T(1024)(128)(4,1)S(1)}, s32[]{:S(2)}) async-start(s8[7340032]{0:T(1024)(128)(4,1)} %bitcast.50), calls=%async_computation.2 | async-start | bytes 6291456
  86.8 12.6 %slice-start.1 = ((s8[7340032]{0:T(1024)(128)(4,1)}), s8[4194304]{0:T(1024)(128)(4,1)S(1)}, s32[]{:S(2)}) async-start(s8[7340032]{0:T(1024)(128)(4,1)} %bitcast.50), calls=%async_computation.3 | async-start | bytes 8388608
  101.6 10.5 %copy-start.3 = (bf16[240,512]{1,0:T(8,128)(2,1)}, bf16[240,512]{1,0:T(8,128)(2,1)S(1)}, u32[]{:S(2)}) copy-start(bf16[240,512]{1,0:T(8,128)(2,1)S(1)} %get-tuple-element.19) | copy-start | bytes 737284
  101.6 10.5 %copy-start.4 = (bf16[240,512]{1,0:T(8,128)(2,1)}, bf16[240,512]{1,0:T(8,128)(2,1)S(1)}, u32[]{:S(2)}) copy-start(bf16[240,512]{1,0:T(8,128)(2,1)S(1)} %get-tuple-element.20) | copy-start | bytes 737284
  101.6 10.5 %copy-start.1 = (bf16[240,512]{1,0:T(8,128)(2,1)}, bf16[240,512]{1,0:T(8,128)(2,1)S(1)}, u32[]{:S(2)}) copy-start(bf16[240,512]{1,0:T(8,128)(2,1)S(1)} %get-tuple-element.21) | copy-start | bytes 737284
  153.9 0.7 copy-start.6
  155.8 8.7 %copy-start.2 = (bf16[240,512]{1,0:T(8,128)(2,1)S(1)}, bf16[240,512]{1,0:T(8,128)(2,1)}, u32[]{:S(2)}) copy-start(bf16[240,512]{1,0:T(8,128)(2,1)} %copy-done.1) | copy-start | bytes 737284
  164.5 5.2 %copy-start.5 = (bf16[240,512]{1,0:T(8,128)(2,1)S(1)}, bf16[240,512]{1,0:T(8,128)(2,1)}, u32[]{:S(2)}) copy-start(bf16[240,512]{1,0:T(8,128)(2,1)} %copy-done.4) | copy-start | bytes 737284
Sparse Core Ops, SparseCore 0:
  19.6 52.4 all-gather.1
  154.1 129.1 all-reduce.2

commit v2 on v1

v2 whole, which is shorter than its diff:
```python
import functools

import jax
import jax.numpy as jnp
from jax import lax
from jax.experimental import pallas as pl
from jax.experimental.pallas import tpu as pltpu
from jax.sharding import PartitionSpec as P

MESH = pl.DeviceIdType.MESH
TILE = 1024
HALF = 32


def contract_last(left, right):
    return lax.dot_general(
        left, right, (((1,), (1,)), ((), ())), preferred_element_type=jnp.float32
    )


def contract_first(left, right):
    return lax.dot_general(
        left, right, (((0,), (0,)), ((), ())), preferred_element_type=jnp.float32
    )


def rows_kernel(chips, counts_ref, tok_ref, cot_ref, wg_hbm, wu_hbm, wd_hbm,
                xs_hbm, acts, own_hbm, back_hbm, ret_hbm,
                wg, wu, wd, x, acc, part_own, part, s_own, s_far,
                w_sem, sib_send, sib_recv, y_send, y_recv, f_send, f_recv,
                po_send, po_recv, ps_send, ps_recv, rt_send, rt_recv, l_sem):
    depth = tok_ref.shape[1]
    slots = tok_ref.shape[0]
    e = lax.axis_index("expert")
    p = lax.axis_index("dp")
    y = p // 2
    c = p % 2
    sibling = (e, y * 2 + 1 - c)

    def chip(step):
        return lax.rem(y + step, chips)

    def rows_at(chip_pos, half, core):
        return pl.ds(pl.multiple_of(((chip_pos * 2 + half) * 2 + core) * HALF, HALF), HALF)

    def columns(k):
        return pl.ds(pl.multiple_of(k * TILE, TILE), TILE)

    loads = [pltpu.make_async_copy(src, dst, w_sem.at[i])
             for i, (src, dst) in enumerate(((wg_hbm, wg), (wu_hbm, wu), (wd_hbm, wd)))]
    for load in loads:
        load.start()

    barrier = pltpu.get_barrier_semaphore()
    pl.semaphore_signal(barrier, inc=1, device_id=sibling, device_id_type=MESH)
    for step in range(1, chips):
        pl.semaphore_signal(barrier, inc=1, device_id=(e, chip(step) * 2 + c), device_id_type=MESH)

    count = counts_ref[e, p]
    first, second = rows_at(y, 0, c), rows_at(y, 1, c)
    tail = pl.ds(pl.multiple_of((y * 4 + 2 + c) * HALF, HALF), slots - HALF)

    @pl.loop(0, depth // TILE)
    def _(k):
        cols = columns(k)
        keep = lax.broadcasted_iota(jnp.int32, (slots, TILE), 0) < count
        for a, ref in enumerate((tok_ref, cot_ref)):
            value = jnp.where(keep, ref[:, cols].astype(jnp.float32), 0.0).astype(jnp.bfloat16)
            x[a, first, cols] = value[:HALF]
            x[a, second, cols] = jnp.zeros((HALF, TILE), jnp.bfloat16)
            x[a, tail, cols] = value[HALF:]

    pl.semaphore_wait(barrier, chips)

    def remote(src, dst, send, recv, device):
        return pltpu.make_async_remote_copy(
            src_ref=src, dst_ref=dst, send_sem=send, recv_sem=recv,
            device_id=device, device_id_type=MESH)

    def to_peer(step, half):
        block = x.at[:, rows_at(y, half, c), :]
        return remote(block, block, y_send.at[step - 1, half], y_recv.at[step - 1, half],
                      (e, chip(step) * 2 + c))

    def to_sibling(half):
        block = x.at[:, rows_at(y, half, c), :]
        return remote(block, block, sib_send.at[half], sib_recv.at[half], sibling)

    def forward(step, half):
        block = x.at[:, rows_at(chip(chips - step), half, c), :]
        return remote(block, block, f_send.at[step - 1, half], f_recv.at[step - 1, half], sibling)

    for half in range(2):
        for step in range(1, chips):
            to_peer(step, half).start()
    for half in range(2):
        to_sibling(half).start()

    def work(row0, count_rows, out):
        rows = pl.ds(pl.multiple_of(row0, 2 * HALF), count_rows)
        acc[:, :count_rows, :] = jnp.zeros((3, count_rows, acc.shape[2]), jnp.float32)

        @pl.loop(0, depth // TILE)
        def _(k):
            cols = columns(k)
            tok, cot = x[0, rows, cols], x[1, rows, cols]
            acc[0, :count_rows] += jnp.dot(tok, wg[cols, :], preferred_element_type=jnp.float32)
            acc[1, :count_rows] += jnp.dot(tok, wu[cols, :], preferred_element_type=jnp.float32)
            acc[2, :count_rows] += contract_last(cot, wd[:, cols])

        gate, up, hidden_grad = acc[0, :count_rows], acc[1, :count_rows], acc[2, :count_rows]
        sigma = jax.nn.sigmoid(gate)
        active = gate * sigma
        acts[0, rows] = (active * up).astype(jnp.bfloat16)
        acts[1, rows] = (hidden_grad * up * (sigma * (1.0 + gate * (1.0 - sigma)))).astype(jnp.bfloat16)
        acts[2, rows] = (hidden_grad * active).astype(jnp.bfloat16)

        @pl.loop(0, depth // TILE)
        def _(k):
            cols = columns(k)
            out[0, :, cols] = jnp.dot(
                acts[0, rows], wd[:, cols], preferred_element_type=jnp.float32).astype(jnp.bfloat16)
            out[1, :, cols] = (contract_last(acts[1, rows], wg[cols, :])
                               + contract_last(acts[2, rows], wu[cols, :])).astype(jnp.bfloat16)

    def add_into(total, term):
        @pl.loop(0, depth // TILE)
        def _(k):
            cols = columns(k)
            total[:, :, cols] = (total[:, :, cols].astype(jnp.float32)
                                 + term[:, :, cols].astype(jnp.float32)).astype(jnp.bfloat16)

    def core_rows(half, core):
        return pl.ds(pl.multiple_of((half * 2 + core) * HALF, HALF), HALF)

    for load in loads:
        load.wait()
    for half in range(2):
        to_sibling(half).wait_recv()
    work(y * 4 * HALF, 4 * HALF, part_own)

    def own_part(half):
        return remote(part_own.at[:, core_rows(half, 1 - c), :], s_own.at[half],
                      po_send.at[half], po_recv.at[half], sibling)

    for half in range(2):
        own_part(half).start()
    for half in range(2):
        own_part(half).wait_recv()
        add_into(s_own.at[half], part_own.at[:, core_rows(half, c), :])
    own_copy = pltpu.make_async_copy(s_own, own_hbm, l_sem.at[0])
    own_copy.start()

    def far_part(step, half, slot):
        return remote(part.at[slot, :, core_rows(0, 1 - c), :], s_far.at[step - 1, half],
                      ps_send.at[step - 1, half], ps_recv.at[step - 1, half], sibling)

    def give_back(step):
        return remote(s_far.at[step - 1, 0], back_hbm.at[step - 1], rt_send.at[step - 1],
                      rt_recv.at[step - 1], (e, chip(chips - step) * 2 + c))

    xs_copy = pltpu.make_async_copy(x, xs_hbm, l_sem.at[1])
    pending = [None, None]
    at = 0
    last = (1, chips - 1)
    for half in range(2):
        for step in range(1, chips):
            to_peer(step, half).wait_recv()
            forward(step, half).start()
            forward(step, half).wait_recv()
            if (half, step) == last:
                xs_copy.start()
            slot = at % 2
            at += 1
            if pending[slot] is not None:
                pending[slot].wait_send()
            work((chip(chips - step) * 2 + half) * 2 * HALF, 2 * HALF, part.at[slot])
            pending[slot] = far_part(step, half, slot)
            pending[slot].start()
            pending[slot].wait_recv()
            add_into(s_far.at[step - 1, half], part.at[slot, :, core_rows(0, c), :])
            if half == 0:
                give_back(step).start()
            else:
                pltpu.make_async_copy(s_far.at[step - 1, 1], ret_hbm.at[step - 1],
                                      l_sem.at[1 + step]).start()
    for transfer in pending:
        if transfer is not None:
            transfer.wait_send()
    for half in range(2):
        to_sibling(half).wait_send()
        own_part(half).wait_send()
        for step in range(1, chips):
            to_peer(step, half).wait_send()
            forward(step, half).wait_send()
    own_copy.wait()
    xs_copy.wait()
    for step in range(1, chips):
        pltpu.make_async_copy(s_far.at[step - 1, 1], ret_hbm.at[step - 1], l_sem.at[1 + step]).wait()
        give_back(step).wait()


def call_rows(chips, counts, tokens, cotangent, gate_w, up_w, down_w):
    depth, width = gate_w.shape
    rows = chips * 4 * HALF
    others = chips - 1
    dtype = jnp.bfloat16
    anywhere = pl.BlockSpec(memory_space=pl.ANY)
    vmem = pl.BlockSpec(memory_space=pltpu.VMEM)
    pairs = pltpu.SemaphoreType.DMA((others, 2))
    halves = pltpu.SemaphoreType.DMA((2,))
    return pl.pallas_call(
        functools.partial(rows_kernel, chips),
        out_shape=(
            jax.ShapeDtypeStruct((2, rows, depth), dtype),
            jax.ShapeDtypeStruct((3, rows, width), dtype),
            jax.ShapeDtypeStruct((2, 2, HALF, depth), dtype),
            jax.ShapeDtypeStruct((others, 2, HALF, depth), dtype),
            jax.ShapeDtypeStruct((others, 2, HALF, depth), dtype),
        ),
        in_specs=[pl.BlockSpec(memory_space=pltpu.SMEM), vmem, vmem, anywhere, anywhere, anywhere],
        out_specs=(anywhere, vmem, anywhere, anywhere, anywhere),
        scratch_shapes=[
            pltpu.VMEM((depth, width), dtype),
            pltpu.VMEM((depth, width), dtype),
            pltpu.VMEM((width, depth), dtype),
            pltpu.VMEM((2, rows, depth), dtype),
            pltpu.VMEM((3, 4 * HALF, width), jnp.float32),
            pltpu.VMEM((2, 4 * HALF, depth), dtype),
            pltpu.VMEM((2, 2, 2 * HALF, depth), dtype),
            pltpu.VMEM((2, 2, HALF, depth), dtype),
            pltpu.VMEM((others, 2, 2, HALF, depth), dtype),
            pltpu.SemaphoreType.DMA((3,)),
            halves, halves, pairs, pairs, pairs, pairs, halves, halves, pairs, pairs,
            pltpu.SemaphoreType.DMA((others,)),
            pltpu.SemaphoreType.DMA((others,)),
            pltpu.SemaphoreType.DMA((2 + others,)),
        ],
        compiler_params=pltpu.CompilerParams(
            collective_id=0, has_side_effects=True, vmem_limit_bytes=60 * 1024 * 1024),
    )(counts, tokens, cotangent, gate_w, up_w, down_w)


def shards(chips, tokens, cotangent, counts, w_gate, w_up, w_down):
    slots = tokens.shape[1]
    xs, acts, own, back, ret = call_rows(
        chips, counts, tokens[0], cotangent[0], w_gate[0], w_up[0], w_down[0])
    got = []
    for step in range(1, chips):
        pairs = [(q * 2 + c, (q - step) % chips * 2 + c) for q in range(chips) for c in range(2)]
        got.append(lax.ppermute(ret[step - 1], "dp", pairs))
    gate_grad = contract_first(xs[0], acts[1]).astype(jnp.bfloat16)
    up_grad = contract_first(xs[0], acts[2]).astype(jnp.bfloat16)
    down_grad = contract_first(acts[0], xs[1]).astype(jnp.bfloat16)
    firsts, seconds = own[0].astype(jnp.float32), own[1].astype(jnp.float32)
    for step in range(1, chips):
        firsts = firsts + back[step - 1].astype(jnp.float32)
        seconds = seconds + got[step - 1].astype(jnp.float32)
    sums = [
        jnp.concatenate([firsts[a], seconds[a, :slots - HALF]], axis=0).astype(jnp.bfloat16)
        for a in range(2)
    ]
    return (sums[0][None], sums[1][None], gate_grad[None], up_grad[None], down_grad[None])


def solution(mesh):
    by_row = P("expert", "dp", None)
    by_column = P("expert", None, "dp")
    return jax.shard_map(
        functools.partial(shards, mesh.shape["dp"] // 2),
        mesh=mesh,
        in_specs=(by_row, by_row, P(), by_column, by_column, by_row),
        out_specs=(by_row, by_row, by_column, by_column, by_row),
        check_vma=False,
    )
```

time: 298 us -> 93 us (0.31)
  waiting for transfers between devices: 161 us -> 2.39 us
  Pallas kernels: 0 us -> 66.8 us
  local copies, waits for them, and re-layouts: 56.7 us -> 1.49 us
  matrix products: 51.1 us -> 17.7 us
  between operations: 14.9 us -> 0.69 us
  other arithmetic: 13.5 us -> 3.42 us
    unnamed x3 -> x0, waiting for transfers between devices: 108 us -> none
    pallas_call x0 -> x1, Pallas kernels: none -> 66.8 us  [call_rows(): pl.pallas_call(functools.partial(rows_kernel, chips), out_shape=(jax.Shap...]
    all_gather x1 -> x0, waiting for transfers between devices: 52.5 us -> none  [shards(): full = lax.all_gather(both, 'dp', axis=1, tiled=True)]
    another operation x1 -> x0, local copies, waits for them, and re-layouts: 32.2 us -> none  [shards(): jnp.stack([out_part.astype(jnp.bfloat16), in_part.astype(jnp.bfloat16)])]
    dot_general x6 -> x0, matrix products: 32.1 us -> none  [the longest x3 17.3 us: contract_last(): lax.dot_general(left, right, (((1,), (1,)), ((), ())), preferred_element_...]
    slice x2, local copies, waits for them, and re-layouts: 18.5 us -> 0.12 us  [the longest x1 0.06 us: shards(): firsts[a]]
    another operation x2, other arithmetic: 7.69 us -> 2.03 us  [the longest x1 5.09 us: shards(): jnp.stack([jnp.where(valid, tokens[0], 0), jnp.where(valid, cotangent[0],...]
    select_n x1 -> x0, other arithmetic: 5.18 us -> none  [shards(): jnp.where(valid, tokens[0], 0)]
  transfers between devices with their start and end apart: 2 -> 1, of which waited for: 2 -> 1; matrix products, arithmetic and copies ran while one was open for 7% -> 21% of each run, Pallas kernels for 0% -> 0%
where the time goes in v2:
time: 93 us; the launch traced here: 92.8 us
  Pallas kernels  66.8 us (72%)
  matrix products  17.7 us (19%)
  other arithmetic  3.42 us (4%)
  waiting for transfers between devices  2.39 us (3%)
  local copies, waits for them, and re-layouts  1.49 us (2%)
    pallas_call x1, Pallas kernels, call_rows(): pl.pallas_call(functools.partial(rows_kernel, chips), out_shape=(jax.Shap...  66.8 us
    dot_general x3, matrix products, contract_first(): lax.dot_general(left, right, (((0,), (0,)), ((), ())), preferred_element_...  17.7 us
    ppermute x1, waiting for transfers between devices, shards(): got.append(lax.ppermute(ret[step - 1], 'dp', pairs))  2.39 us
    another operation x2, other arithmetic  2.03 us
  transfers between devices with their start and end apart: 1, of which 1 were waited for; matrix products, arithmetic and copies ran while one was open for 21% of the time, Pallas kernels for 0%

profile of v2, /device:TPU:0, one launch (start us, length us, event | category | flops | bytes accessed | tf_op | source)
XLA Modules:
  0.0 92.8 jit_solution(3465660452682646557)
XLA Ops:
  0.6 1.3 %copy.11.counts_ref = s32[8,4]{1,0:T(8,128)} copy(s32[8,4]{0,1:T(4,128)} %param.8) | data formatting | bytes 256 | tf_op args[2]
  2.0 66.8 %shard_map.101 = (bf16[2,256,7168]{2,1,0:T(8,128)(2,1)}, bf16[3,256,512]{2,1,0:T(8,128)(2,1)}, bf16[2,2,32,7168]{3,2,1,0:T(8,128)(2,1)}, bf16[1,2,32,7168]{3,2,1,0:T(8,128)(2,1)}, bf16[1,2,32,7168]{3,2,1,0:T(8,128)(2,1)}) custom-call(s32[8,4]{1,0:T(8,128)} %copy.11.counts_ref, bf16[60,7168]{1,0:T(8,128)(2,1)} %bitcast.41, bf16[60,7168]{1,0:T(8,128)(2,1)} %bitcast.42, ...), custom_call_target="tpu_custom_call" | custom-call | tf_op jit(solution)/shard_map/pallas_call | solution.py:212
  68.8 0.0 copy-start.1
  68.8 0.4 collective-permute-start
  69.2 0.0 slice-start
  69.2 1.8 %add_convert_fusion = bf16[1,2,32,7168]{3,2,1,0:T(8,128)(2,1)S(1)} fusion(bf16[1,2,32,7168]{3,2,1,0:T(8,128)(2,1)} %get-tuple-element.11, bf16[2,2,32,7168]{3,2,1,0:T(8,128)(2,1)} %get-tuple-element.10), kind=kLoop, calls=%fused_computation.14 | loop fusion | flops 1835008 | bytes 2752512 | tf_op jit(solution)/shard_map/convert.10
  71.0 0.1 slice_bitcast_fusion
  71.1 0.0 copy-done.1
  71.1 0.0 slice-start.1
  71.1 7.3 %fusion.2 = bf16[1,512,7168]{2,1,0:T(8,128)(2,1)} fusion(bf16[2,256,7168]{2,1,0:T(8,128)(2,1)} %get-tuple-element.13, bf16[3,256,512]{2,1,0:T(8,128)(2,1)S(1)} %copy-done.1), kind=kOutput, calls=%fused_computation.5 | convolution fusion | flops 1882718208 | bytes 11272192 | tf_op jit(solution)/shard_map/dot_general | solution.py:22
  78.4 0.0 slice-done
  78.4 0.0 slice-done.1
  78.4 5.2 %fusion.1 = bf16[1,7168,512]{2,1,0:T(8,128)(2,1)} fusion(bf16[2,256,7168]{2,1,0:T(8,128)(2,1)S(1)} %bitcast.40, bf16[3,256,512]{2,1,0:T(8,128)(2,1)S(1)} %copy-done.1), kind=kOutput, calls=%fused_computation.4 | convolution fusion | flops 1882718208 | bytes 11272192 | tf_op jit(solution)/shard_map/dot_general | solution.py:22
  83.6 0.0 copy-start
  83.6 5.2 %fusion = bf16[1,7168,512]{2,1,0:T(8,128)(2,1)} fusion(bf16[2,256,7168]{2,1,0:T(8,128)(2,1)S(1)} %bitcast.40, bf16[3,256,512]{2,1,0:T(8,128)(2,1)S(1)} %copy-done.1), kind=kOutput, calls=%fused_computation.3 | convolution fusion | flops 1882718208 | bytes 11272192 | tf_op jit(solution)/shard_map/dot_general | solution.py:22
  88.8 2.4 %collective-permute-done = bf16[2,32,7168]{2,1,0:T(8,128)(2,1)S(1)} collective-permute-done((bf16[2,32,7168]{2,1,0:T(8,128)(2,1)}, bf16[2,32,7168]{2,1,0:T(8,128)(2,1)S(1)}, u32[]{:S(2)}, u32[]{:S(2)}) %collective-permute-start) | collective-permute-done | bytes 917536 | tf_op jit(solution)/shard_map/ppermute | solution.py:251
  91.1 0.0 copy-done
  91.1 0.2 fusion.9
  91.4 0.1 fusion.16
  91.4 1.4 %pad_maximum_fusion = (bf16[1,60,7168]{2,1,0:T(8,128)(2,1)}, bf16[1,60,7168]{2,1,0:T(8,128)(2,1)}) fusion(bf16[1,28,7168]{2,1,0:T(8,128)(2,1)S(1)} %get-tuple-element.18, bf16[1,32,7168]{2,1,0:T(8,128)(2,1)S(1)} %get-tuple-element.16, bf16[1,28,7168]{2,1,0:T(8,128)(2,1)S(1)} %get-tuple-element.17, bf16[1,32,7168]{2,1,0:T(8,128)(2,1)S(1)} %get-tuple-element.15), kind=kLoop, calls=%fused_computation.15 | loop fusion | flops 3440640 | bytes 3440640 | tf_op jit(solution)/shard_map/concatenate | solution.py:260
  (1 shorter events, 0.0 us)
Async XLA Ops:
  68.8 2.3 %copy-start.1 = (bf16[3,256,512]{2,1,0:T(8,128)(2,1)S(1)}, bf16[3,256,512]{2,1,0:T(8,128)(2,1)}, u32[]{:S(2)}) copy-start(bf16[3,256,512]{2,1,0:T(8,128)(2,1)} %get-tuple-element.14) | copy-start | bytes 2359300
  68.8 22.4 %collective-permute-start = (bf16[2,32,7168]{2,1,0:T(8,128)(2,1)}, bf16[2,32,7168]{2,1,0:T(8,128)(2,1)S(1)}, u32[]{:S(2)}, u32[]{:S(2)}) collective-permute-start(bf16[2,32,7168]{2,1,0:T(8,128)(2,1)} %bitcast.43), channel_id=1, source_target_pairs={{0,2},{1,3},{2,0},{3,1},{4,6},{5,7},{6,4},{7,5},{8,10},{9,11},{10,... | collective-permute-start | bytes 2752520 | tf_op jit(solution)/shard_map/ppermute | solution.py:251
  69.2 9.3 %slice-start = ((s8[7340032]{0:T(1024)(128)(4,1)}), s8[4194304]{0:T(1024)(128)(4,1)S(1)}, s32[]{:S(2)}) async-start(s8[7340032]{0:T(1024)(128)(4,1)} %bitcast.39), calls=%async_computation | async-start | bytes 8388608
  71.1 7.4 %slice-start.1 = ((s8[7340032]{0:T(1024)(128)(4,1)}), s8[3145728]{0:T(1024)(128)(4,1)S(1)}, s32[]{:S(2)}) async-start(s8[7340032]{0:T(1024)(128)(4,1)} %bitcast.39), calls=%async_computation.1 | async-start | bytes 6291456
  83.6 7.5 %copy-start = (bf16[2,2,32,7168]{3,2,1,0:T(8,128)(2,1)S(1)}, bf16[2,2,32,7168]{3,2,1,0:T(8,128)(2,1)}, u32[]{:S(2)}) copy-start(bf16[2,2,32,7168]{3,2,1,0:T(8,128)(2,1)} %get-tuple-element.10) | copy-start | bytes 5505028

commit v3 on v2

--- a/solution.py
+++ b/solution.py
@@ -10,6 +10,7 @@
 MESH = pl.DeviceIdType.MESH
 TILE = 1024
 HALF = 32
+SIDE = 512
 
 
 def contract_last(left, right):
@@ -26,9 +27,9 @@
 
 def rows_kernel(chips, counts_ref, tok_ref, cot_ref, wg_hbm, wu_hbm, wd_hbm,
                 xs_hbm, acts, own_hbm, back_hbm, ret_hbm,
-                wg, wu, wd, x, acc, part_own, part, s_own, s_far,
+                wg, wu, wd, x, acc, part_own, part, s_own, s_far, pk, pk_got, rp, rp_got,
                 w_sem, sib_send, sib_recv, y_send, y_recv, f_send, f_recv,
-                po_send, po_recv, ps_send, ps_recv, rt_send, rt_recv, l_sem):
+                po_send, po_recv, ps_send, ps_recv, rt_send, rt_recv, k_send, k_recv, l_sem):
     depth = tok_ref.shape[1]
     slots = tok_ref.shape[0]
     e = lax.axis_index("expert")
@@ -56,21 +57,74 @@
     for step in range(1, chips):
         pl.semaphore_signal(barrier, inc=1, device_id=(e, chip(step) * 2 + c), device_id_type=MESH)
 
-    count = counts_ref[e, p]
-    first, second = rows_at(y, 0, c), rows_at(y, 1, c)
-    tail = pl.ds(pl.multiple_of((y * 4 + 2 + c) * HALF, HALF), slots - HALF)
-
-    @pl.loop(0, depth // TILE)
-    def _(k):
-        cols = columns(k)
-        keep = lax.broadcasted_iota(jnp.int32, (slots, TILE), 0) < count
-        for a, ref in enumerate((tok_ref, cot_ref)):
-            value = jnp.where(keep, ref[:, cols].astype(jnp.float32), 0.0).astype(jnp.bfloat16)
-            x[a, first, cols] = value[:HALF]
-            x[a, second, cols] = jnp.zeros((HALF, TILE), jnp.bfloat16)
-            x[a, tail, cols] = value[HALF:]
-
-    pl.semaphore_wait(barrier, chips)
+    table = counts_ref[...]
+    here = jnp.logical_and(lax.broadcasted_iota(jnp.int32, table.shape, 0) == e,
+                           lax.broadcasted_iota(jnp.int32, table.shape, 1) == p)
+    picked = jnp.where(here, table.astype(jnp.float32), 0.0)
+    count = jnp.sum(jnp.sum(picked, axis=1, keepdims=True), axis=0, keepdims=True)
+
+    def mask_half(half):
+        filled = min(HALF, slots - half * HALF)
+        start = ((y * 2 + half) * 2 + c) * HALF
+        rows = pl.ds(pl.multiple_of(start, HALF), filled)
+
+        @pl.loop(0, depth // TILE)
+        def _(k):
+            cols = columns(k)
+            slot = (lax.broadcasted_iota(jnp.int32, (filled, TILE), 0) + half * HALF).astype(jnp.float32)
+            keep = slot < count
+            for a, ref in enumerate((tok_ref, cot_ref)):
+                value = ref[half * HALF:half * HALF + filled, cols].astype(jnp.float32)
+                if filled < HALF:
+                    x[a, rows_at(y, half, c), cols] = jnp.zeros((HALF, TILE), jnp.bfloat16)
+                x[a, rows, cols] = jnp.where(keep, value, 0.0).astype(jnp.bfloat16)
+
+    extra = slots - HALF - 16
+    middle = depth // 2
+
+    def selection(side, transposed):
+        shape = (32, 4 * extra) if transposed else (4 * extra, 32)
+        packed = lax.broadcasted_iota(jnp.int32, shape, 1 if transposed else 0)
+        row = lax.broadcasted_iota(jnp.int32, shape, 0 if transposed else 1)
+        hit = None
+        for a in range(2):
+            start = (2 * a + side) * extra
+            inside = jnp.logical_and(packed >= start, packed < start + extra)
+            match = jnp.logical_and(inside, packed - start == row - 16 * a)
+            hit = match if hit is None else jnp.logical_or(hit, match)
+        return jnp.where(hit, 1.0, 0.0).astype(jnp.bfloat16)
+
+    def side_columns(side, k):
+        return pl.ds(pl.multiple_of(side * middle + k * SIDE, SIDE), SIDE)
+
+    def pack(src, rows, dst):
+        picks = [selection(side, False) for side in range(2)]
+
+        @pl.loop(0, middle // SIDE)
+        def _(k):
+            total = None
+            for side in range(2):
+                cols = side_columns(side, k)
+                both = jnp.concatenate([src[0, rows, cols], src[1, rows, cols]], axis=0)
+                term = jnp.dot(picks[side], both, preferred_element_type=jnp.float32)
+                total = term if total is None else total + term
+            dst[:, side_columns(0, k)] = total.astype(jnp.bfloat16)
+
+    def unpack(src, dst, rows):
+        picks = [selection(side, True) for side in range(2)]
+
+        @pl.loop(0, middle // SIDE)
+        def _(k):
+            value = src[:, side_columns(0, k)]
+            for side in range(2):
+                cols = side_columns(side, k)
+                both = jnp.dot(picks[side], value, preferred_element_type=jnp.float32).astype(jnp.bfloat16)
+                dst[0, rows, cols] = both[:16]
+                dst[1, rows, cols] = both[16:]
+
+    def sixteen(chip_pos, core, part_of):
+        start = ((chip_pos * 2 + 1) * 2 + core) * HALF + part_of * 16
+        return pl.ds(pl.multiple_of(start, 16), 16)
 
     def remote(src, dst, send, recv, device):
         return pltpu.make_async_remote_copy(
@@ -78,8 +132,12 @@
             device_id=device, device_id_type=MESH)
 
     def to_peer(step, half):
-        block = x.at[:, rows_at(y, half, c), :]
+        block = x.at[:, sixteen(y, c, 0) if half else rows_at(y, half, c), :]
         return remote(block, block, y_send.at[step - 1, half], y_recv.at[step - 1, half],
+                      (e, chip(step) * 2 + c))
+
+    def tail_to_peer(step):
+        return remote(pk, pk_got.at[step - 1], k_send.at[step - 1, 0], k_recv.at[step - 1, 0],
                       (e, chip(step) * 2 + c))
 
     def to_sibling(half):
@@ -90,9 +148,16 @@
         block = x.at[:, rows_at(chip(chips - step), half, c), :]
         return remote(block, block, f_send.at[step - 1, half], f_recv.at[step - 1, half], sibling)
 
-    for half in range(2):
-        for step in range(1, chips):
-            to_peer(step, half).start()
+    mask_half(1)
+    pl.semaphore_wait(barrier, chips)
+    for step in range(1, chips):
+        to_peer(step, 1).start()
+    pack(x, sixteen(y, c, 1), pk)
+    for step in range(1, chips):
+        tail_to_peer(step).start()
+    mask_half(0)
+    for step in range(1, chips):
+        to_peer(step, 0).start()
     for half in range(2):
         to_sibling(half).start()
 
@@ -156,16 +221,30 @@
                       ps_send.at[step - 1, half], ps_recv.at[step - 1, half], sibling)
 
     def give_back(step):
-        return remote(s_far.at[step - 1, 0], back_hbm.at[step - 1], rt_send.at[step - 1],
-                      rt_recv.at[step - 1], (e, chip(chips - step) * 2 + c))
+        return remote(s_far.at[step - 1, 1, :, 0:16, :], back_hbm.at[step - 1, :, 0:16, :],
+                      rt_send.at[step - 1], rt_recv.at[step - 1], (e, chip(chips - step) * 2 + c))
+
+    def tail_back(step):
+        return remote(rp.at[step - 1], rp_got.at[step - 1], k_send.at[step - 1, 1], k_recv.at[step - 1, 1],
+                      (e, chip(chips - step) * 2 + c))
+
+    def back_copy(step):
+        return pltpu.make_async_copy(s_far.at[step - 1, 1, :, 16:32, :],
+                                     back_hbm.at[step - 1, :, 16:32, :], l_sem.at[1 + chips + step - 1])
+
+    def ret_copy(step):
+        return pltpu.make_async_copy(s_far.at[step - 1, 0], ret_hbm.at[step - 1], l_sem.at[1 + step])
 
     xs_copy = pltpu.make_async_copy(x, xs_hbm, l_sem.at[1])
     pending = [None, None]
     at = 0
-    last = (1, chips - 1)
-    for half in range(2):
+    last = (0, chips - 1)
+    for half in (1, 0):
         for step in range(1, chips):
             to_peer(step, half).wait_recv()
+            if half:
+                tail_to_peer(step).wait_recv()
+                unpack(pk_got.at[step - 1], x, sixteen(chip(chips - step), c, 1))
             forward(step, half).start()
             forward(step, half).wait_recv()
             if (half, step) == last:
@@ -179,11 +258,12 @@
             pending[slot].start()
             pending[slot].wait_recv()
             add_into(s_far.at[step - 1, half], part.at[slot, :, core_rows(0, c), :])
-            if half == 0:
+            if half:
                 give_back(step).start()
+                pack(s_far.at[step - 1, 1], pl.ds(16, 16), rp.at[step - 1])
+                tail_back(step).start()
             else:
-                pltpu.make_async_copy(s_far.at[step - 1, 1], ret_hbm.at[step - 1],
-                                      l_sem.at[1 + step]).start()
+                ret_copy(step).start()
     for transfer in pending:
         if transfer is not None:
             transfer.wait_send()
@@ -196,14 +276,21 @@
     own_copy.wait()
     xs_copy.wait()
     for step in range(1, chips):
-        pltpu.make_async_copy(s_far.at[step - 1, 1], ret_hbm.at[step - 1], l_sem.at[1 + step]).wait()
+        tail_to_peer(step).wait_send()
+        ret_copy(step).wait()
         give_back(step).wait()
+        tail_back(step).wait()
+        unpack(rp_got.at[step - 1], s_far.at[step - 1, 1], pl.ds(16, 16))
+        back_copy(step).start()
+    for step in range(1, chips):
+        back_copy(step).wait()
 
 
 def call_rows(chips, counts, tokens, cotangent, gate_w, up_w, down_w):
     depth, width = gate_w.shape
     rows = chips * 4 * HALF
     others = chips - 1
+    tail = (4 * (tokens.shape[0] - HALF - 16), depth // 2)
     dtype = jnp.bfloat16
     anywhere = pl.BlockSpec(memory_space=pl.ANY)
     vmem = pl.BlockSpec(memory_space=pltpu.VMEM)
@@ -218,7 +305,7 @@
             jax.ShapeDtypeStruct((others, 2, HALF, depth), dtype),
             jax.ShapeDtypeStruct((others, 2, HALF, depth), dtype),
         ),
-        in_specs=[pl.BlockSpec(memory_space=pltpu.SMEM), vmem, vmem, anywhere, anywhere, anywhere],
+        in_specs=[vmem, vmem, vmem, anywhere, anywhere, anywhere],
         out_specs=(anywhere, vmem, anywhere, anywhere, anywhere),
         scratch_shapes=[
             pltpu.VMEM((depth, width), dtype),
@@ -230,11 +317,16 @@
             pltpu.VMEM((2, 2, 2 * HALF, depth), dtype),
             pltpu.VMEM((2, 2, HALF, depth), dtype),
             pltpu.VMEM((others, 2, 2, HALF, depth), dtype),
+            pltpu.VMEM(tail, dtype),
+            pltpu.VMEM((others,) + tail, dtype),
+            pltpu.VMEM((others,) + tail, dtype),
+            pltpu.VMEM((others,) + tail, dtype),
             pltpu.SemaphoreType.DMA((3,)),
             halves, halves, pairs, pairs, pairs, pairs, halves, halves, pairs, pairs,
             pltpu.SemaphoreType.DMA((others,)),
             pltpu.SemaphoreType.DMA((others,)),
-            pltpu.SemaphoreType.DMA((2 + others,)),
+            pairs, pairs,
+            pltpu.SemaphoreType.DMA((2 + 2 * others,)),
         ],
         compiler_params=pltpu.CompilerParams(
             collective_id=0, has_side_effects=True, vmem_limit_bytes=60 * 1024 * 1024),
@@ -254,8 +346,8 @@
     down_grad = contract_first(acts[0], xs[1]).astype(jnp.bfloat16)
     firsts, seconds = own[0].astype(jnp.float32), own[1].astype(jnp.float32)
     for step in range(1, chips):
-        firsts = firsts + back[step - 1].astype(jnp.float32)
-        seconds = seconds + got[step - 1].astype(jnp.float32)
+        firsts = firsts + got[step - 1].astype(jnp.float32)
+        seconds = seconds + back[step - 1].astype(jnp.float32)
     sums = [
         jnp.concatenate([firsts[a], seconds[a, :slots - HALF]], axis=0).astype(jnp.bfloat16)
         for a in range(2)

time: 93 us -> 93.7 us (level)
  no operation moved by 1% of the time
where the time goes in v3:
time: 93.7 us; the launch traced here: 93.5 us
  Pallas kernels  67.2 us (72%)
  matrix products  17.7 us (19%)
  other arithmetic  3.42 us (4%)
  waiting for transfers between devices  2.69 us (3%)
  local copies, waits for them, and re-layouts  1.49 us (2%)
    pallas_call x1, Pallas kernels, call_rows(): pl.pallas_call(functools.partial(rows_kernel, chips), out_shape=(jax.Shap...  67.2 us
    dot_general x3, matrix products, contract_first(): lax.dot_general(left, right, (((0,), (0,)), ((), ())), preferred_element_...  17.7 us
    ppermute x1, waiting for transfers between devices, shards(): got.append(lax.ppermute(ret[step - 1], 'dp', pairs))  2.69 us
    another operation x2, other arithmetic  2.03 us
  transfers between devices with their start and end apart: 1, of which 1 were waited for; matrix products, arithmetic and copies ran while one was open for 21% of the time, Pallas kernels for 0%

profile of v3, /device:TPU:0, one launch (start us, length us, event | category | flops | bytes accessed | tf_op | source)
XLA Modules:
  0.0 93.5 jit_solution(10896281859063930888)
XLA Ops:
  0.6 1.3 %copy.11.counts_ref = s32[8,4]{1,0:T(8,128)} copy(s32[8,4]{0,1:T(4,128)} %param.8) | data formatting | bytes 256 | tf_op args[2]
  2.0 67.2 %shard_map.101 = (bf16[2,256,7168]{2,1,0:T(8,128)(2,1)}, bf16[3,256,512]{2,1,0:T(8,128)(2,1)}, bf16[2,2,32,7168]{3,2,1,0:T(8,128)(2,1)}, bf16[1,2,32,7168]{3,2,1,0:T(8,128)(2,1)}, bf16[1,2,32,7168]{3,2,1,0:T(8,128)(2,1)}) custom-call(s32[8,4]{1,0:T(8,128)} %copy.11.counts_ref, bf16[60,7168]{1,0:T(8,128)(2,1)} %bitcast.39, bf16[60,7168]{1,0:T(8,128)(2,1)} %bitcast.40, ...), custom_call_target="tpu_custom_call" | custom-call | tf_op jit(solution)/shard_map/pallas_call | solution.py:299
  69.2 0.0 copy-start.1
  69.2 0.3 collective-permute-start
  69.6 0.0 slice-start
  69.6 1.8 %fusion.10 = bf16[2,32,7168]{2,1,0:T(8,128)(2,1)S(1)} fusion(bf16[1,2,32,7168]{3,2,1,0:T(8,128)(2,1)} %get-tuple-element.12, bf16[2,2,32,7168]{3,2,1,0:T(8,128)(2,1)} %get-tuple-element.10), kind=kLoop, calls=%fused_computation.15 | loop fusion | flops 1835008 | bytes 2752512 | tf_op jit(solution)/shard_map/convert.7
  71.4 0.1 fusion.18
  71.5 0.0 copy-done.1
  71.5 0.0 slice-start.1
  71.5 7.3 %fusion.2 = bf16[1,512,7168]{2,1,0:T(8,128)(2,1)} fusion(bf16[2,256,7168]{2,1,0:T(8,128)(2,1)} %get-tuple-element.13, bf16[3,256,512]{2,1,0:T(8,128)(2,1)S(1)} %copy-done.1), kind=kOutput, calls=%fused_computation.5 | convolution fusion | flops 1882718208 | bytes 11272192 | tf_op jit(solution)/shard_map/dot_general | solution.py:23
  78.8 0.0 slice-done
  78.8 0.0 slice-done.1
  78.8 5.2 %fusion.1 = bf16[1,7168,512]{2,1,0:T(8,128)(2,1)} fusion(bf16[2,256,7168]{2,1,0:T(8,128)(2,1)S(1)} %bitcast.38, bf16[3,256,512]{2,1,0:T(8,128)(2,1)S(1)} %copy-done.1), kind=kOutput, calls=%fused_computation.4 | convolution fusion | flops 1882718208 | bytes 11272192 | tf_op jit(solution)/shard_map/dot_general | solution.py:23
  84.0 0.0 copy-start
  84.0 5.2 %fusion = bf16[1,7168,512]{2,1,0:T(8,128)(2,1)} fusion(bf16[2,256,7168]{2,1,0:T(8,128)(2,1)S(1)} %bitcast.38, bf16[3,256,512]{2,1,0:T(8,128)(2,1)S(1)} %copy-done.1), kind=kOutput, calls=%fused_computation.3 | convolution fusion | flops 1882718208 | bytes 11272192 | tf_op jit(solution)/shard_map/dot_general | solution.py:23
  89.1 2.7 %collective-permute-done = bf16[2,32,7168]{2,1,0:T(8,128)(2,1)S(1)} collective-permute-done((bf16[2,32,7168]{2,1,0:T(8,128)(2,1)}, bf16[2,32,7168]{2,1,0:T(8,128)(2,1)S(1)}, u32[]{:S(2)}, u32[]{:S(2)}) %collective-permute-start) | collective-permute-done | bytes 917536 | tf_op jit(solution)/shard_map/ppermute | solution.py:343
  91.8 0.0 copy-done
  91.8 0.2 fusion.9
  92.1 0.1 fusion.17
  92.1 1.4 %pad_maximum_fusion = (bf16[1,60,7168]{2,1,0:T(8,128)(2,1)}, bf16[1,60,7168]{2,1,0:T(8,128)(2,1)}) fusion(bf16[1,28,7168]{2,1,0:T(8,128)(2,1)S(1)} %get-tuple-element.18, bf16[1,32,7168]{2,1,0:T(8,128)(2,1)S(1)} %get-tuple-element.16, bf16[1,28,7168]{2,1,0:T(8,128)(2,1)S(1)} %get-tuple-element.17, bf16[1,32,7168]{2,1,0:T(8,128)(2,1)S(1)} %get-tuple-element.15), kind=kLoop, calls=%fused_computation.16 | loop fusion | flops 3440640 | bytes 3440640 | tf_op jit(solution)/shard_map/concatenate | solution.py:352
  (1 shorter events, 0.0 us)
Async XLA Ops:
  69.2 2.2 %copy-start.1 = (bf16[3,256,512]{2,1,0:T(8,128)(2,1)S(1)}, bf16[3,256,512]{2,1,0:T(8,128)(2,1)}, u32[]{:S(2)}) copy-start(bf16[3,256,512]{2,1,0:T(8,128)(2,1)} %get-tuple-element.14) | copy-start | bytes 2359300
  69.2 22.6 %collective-permute-start = (bf16[2,32,7168]{2,1,0:T(8,128)(2,1)}, bf16[2,32,7168]{2,1,0:T(8,128)(2,1)S(1)}, u32[]{:S(2)}, u32[]{:S(2)}) collective-permute-start(bf16[2,32,7168]{2,1,0:T(8,128)(2,1)} %bitcast.41), channel_id=1, source_target_pairs={{0,2},{1,3},{2,0},{3,1},{4,6},{5,7},{6,4},{7,5},{8,10},{9,11},{10,... | collective-permute-start | bytes 2752520 | tf_op jit(solution)/shard_map/ppermute | solution.py:343
  69.6 9.3 %slice-start = ((s8[7340032]{0:T(1024)(128)(4,1)}), s8[4194304]{0:T(1024)(128)(4,1)S(1)}, s32[]{:S(2)}) async-start(s8[7340032]{0:T(1024)(128)(4,1)} %bitcast.37), calls=%async_computation | async-start | bytes 8388608
  71.5 7.4 %slice-start.1 = ((s8[7340032]{0:T(1024)(128)(4,1)}), s8[3145728]{0:T(1024)(128)(4,1)S(1)}, s32[]{:S(2)}) async-start(s8[7340032]{0:T(1024)(128)(4,1)} %bitcast.37), calls=%async_computation.1 | async-start | bytes 6291456
  84.0 7.9 %copy-start = (bf16[2,2,32,7168]{3,2,1,0:T(8,128)(2,1)S(1)}, bf16[2,2,32,7168]{3,2,1,0:T(8,128)(2,1)}, u32[]{:S(2)}) copy-start(bf16[2,2,32,7168]{3,2,1,0:T(8,128)(2,1)} %get-tuple-element.10) | copy-start | bytes 5505028

commit v4 on v3

--- a/solution.py
+++ b/solution.py
@@ -210,11 +210,6 @@
 
     for half in range(2):
         own_part(half).start()
-    for half in range(2):
-        own_part(half).wait_recv()
-        add_into(s_own.at[half], part_own.at[:, core_rows(half, c), :])
-    own_copy = pltpu.make_async_copy(s_own, own_hbm, l_sem.at[0])
-    own_copy.start()
 
     def far_part(step, half, slot):
         return remote(part.at[slot, :, core_rows(0, 1 - c), :], s_far.at[step - 1, half],
@@ -264,6 +259,11 @@
                 tail_back(step).start()
             else:
                 ret_copy(step).start()
+    for half in range(2):
+        own_part(half).wait_recv()
+        add_into(s_own.at[half], part_own.at[:, core_rows(half, c), :])
+    own_copy = pltpu.make_async_copy(s_own, own_hbm, l_sem.at[0])
+    own_copy.start()
     for transfer in pending:
         if transfer is not None:
             transfer.wait_send()

time: 93.7 us -> 91.1 us (0.972)
  Pallas kernels: 67.2 us -> 64.6 us
  waiting for transfers between devices: 2.69 us -> 0.99 us
  starting transfers between devices: 0.35 us -> 2.01 us
    pallas_call x1, Pallas kernels: 67.2 us -> 64.6 us  [call_rows(): pl.pallas_call(functools.partial(rows_kernel, chips), out_shape=(jax.Shap...]
    ppermute x1, waiting for transfers between devices: 2.69 us -> 0.99 us  [shards(): got.append(lax.ppermute(ret[step - 1], 'dp', pairs))]
    ppermute x1, starting transfers between devices: 0.35 us -> 2.01 us  [shards(): got.append(lax.ppermute(ret[step - 1], 'dp', pairs))]
where the time goes in v4:
time: 91.1 us; the launch traced here: 90.9 us
  Pallas kernels  64.6 us (71%)
  matrix products  17.7 us (19%)
  other arithmetic  3.42 us (4%)
  starting transfers between devices  2.01 us (2%)
  local copies, waits for them, and re-layouts  1.49 us (2%)
  waiting for transfers between devices  0.99 us (1%)
    pallas_call x1, Pallas kernels, call_rows(): pl.pallas_call(functools.partial(rows_kernel, chips), out_shape=(jax.Shap...  64.6 us
    dot_general x3, matrix products, contract_first(): lax.dot_general(left, right, (((0,), (0,)), ((), ())), preferred_element_...  17.7 us
    another operation x2, other arithmetic  2.03 us
    ppermute x1, starting transfers between devices, shards(): got.append(lax.ppermute(ret[step - 1], 'dp', pairs))  2.01 us
  transfers between devices with their start and end apart: 1, of which 1 were waited for; matrix products, arithmetic and copies ran while one was open for 21% of the time, Pallas kernels for 0%

profile of v4, /device:TPU:0, one launch (start us, length us, event | category | flops | bytes accessed | tf_op | source)
XLA Modules:
  0.0 90.9 jit_solution(5832722111028653952)
XLA Ops:
  0.6 1.3 %copy.11.counts_ref = s32[8,4]{1,0:T(8,128)} copy(s32[8,4]{0,1:T(4,128)} %param.8) | data formatting | bytes 256 | tf_op args[2]
  2.0 64.6 %shard_map.101 = (bf16[2,256,7168]{2,1,0:T(8,128)(2,1)}, bf16[3,256,512]{2,1,0:T(8,128)(2,1)}, bf16[2,2,32,7168]{3,2,1,0:T(8,128)(2,1)}, bf16[1,2,32,7168]{3,2,1,0:T(8,128)(2,1)}, bf16[1,2,32,7168]{3,2,1,0:T(8,128)(2,1)}) custom-call(s32[8,4]{1,0:T(8,128)} %copy.11.counts_ref, bf16[60,7168]{1,0:T(8,128)(2,1)} %bitcast.39, bf16[60,7168]{1,0:T(8,128)(2,1)} %bitcast.40, ...), custom_call_target="tpu_custom_call" | custom-call | tf_op jit(solution)/shard_map/pallas_call | solution.py:299
  66.6 0.0 copy-start.1
  66.6 2.0 %collective-permute-start = (bf16[2,32,7168]{2,1,0:T(8,128)(2,1)}, bf16[2,32,7168]{2,1,0:T(8,128)(2,1)S(1)}, u32[]{:S(2)}, u32[]{:S(2)}) collective-permute-start(bf16[2,32,7168]{2,1,0:T(8,128)(2,1)} %bitcast.41), channel_id=1, source_target_pairs={{0,2},{1,3},{2,0},{3,1},{4,6},{5,7},{6,4},{7,5},{8,10},{9,11},{10,... | collective-permute-start | bytes 2752520 | tf_op jit(solution)/shard_map/ppermute | solution.py:343
  68.7 0.0 slice-start
  68.7 1.8 %fusion.10 = bf16[2,32,7168]{2,1,0:T(8,128)(2,1)S(1)} fusion(bf16[1,2,32,7168]{3,2,1,0:T(8,128)(2,1)} %get-tuple-element.12, bf16[2,2,32,7168]{3,2,1,0:T(8,128)(2,1)} %get-tuple-element.10), kind=kLoop, calls=%fused_computation.15 | loop fusion | flops 1835008 | bytes 2752512 | tf_op jit(solution)/shard_map/convert.7
  70.5 0.1 fusion.18
  70.5 0.0 copy-done.1
  70.6 0.0 slice-start.1
  70.6 7.3 %fusion.2 = bf16[1,512,7168]{2,1,0:T(8,128)(2,1)} fusion(bf16[2,256,7168]{2,1,0:T(8,128)(2,1)} %get-tuple-element.13, bf16[3,256,512]{2,1,0:T(8,128)(2,1)S(1)} %copy-done.1), kind=kOutput, calls=%fused_computation.5 | convolution fusion | flops 1882718208 | bytes 11272192 | tf_op jit(solution)/shard_map/dot_general | solution.py:23
  77.9 0.0 slice-done
  77.9 0.0 slice-done.1
  77.9 5.2 %fusion.1 = bf16[1,7168,512]{2,1,0:T(8,128)(2,1)} fusion(bf16[2,256,7168]{2,1,0:T(8,128)(2,1)S(1)} %bitcast.38, bf16[3,256,512]{2,1,0:T(8,128)(2,1)S(1)} %copy-done.1), kind=kOutput, calls=%fused_computation.4 | convolution fusion | flops 1882718208 | bytes 11272192 | tf_op jit(solution)/shard_map/dot_general | solution.py:23
  83.1 0.0 copy-start
  83.1 5.2 %fusion = bf16[1,7168,512]{2,1,0:T(8,128)(2,1)} fusion(bf16[2,256,7168]{2,1,0:T(8,128)(2,1)S(1)} %bitcast.38, bf16[3,256,512]{2,1,0:T(8,128)(2,1)S(1)} %copy-done.1), kind=kOutput, calls=%fused_computation.3 | convolution fusion | flops 1882718208 | bytes 11272192 | tf_op jit(solution)/shard_map/dot_general | solution.py:23
  88.2 1.0 %collective-permute-done = bf16[2,32,7168]{2,1,0:T(8,128)(2,1)S(1)} collective-permute-done((bf16[2,32,7168]{2,1,0:T(8,128)(2,1)}, bf16[2,32,7168]{2,1,0:T(8,128)(2,1)S(1)}, u32[]{:S(2)}, u32[]{:S(2)}) %collective-permute-start) | collective-permute-done | bytes 917536 | tf_op jit(solution)/shard_map/ppermute | solution.py:343
  89.2 0.0 copy-done
  89.2 0.2 fusion.9
  89.4 0.1 fusion.17
  89.5 1.4 %pad_maximum_fusion = (bf16[1,60,7168]{2,1,0:T(8,128)(2,1)}, bf16[1,60,7168]{2,1,0:T(8,128)(2,1)}) fusion(bf16[1,28,7168]{2,1,0:T(8,128)(2,1)S(1)} %get-tuple-element.18, bf16[1,32,7168]{2,1,0:T(8,128)(2,1)S(1)} %get-tuple-element.16, bf16[1,28,7168]{2,1,0:T(8,128)(2,1)S(1)} %get-tuple-element.17, bf16[1,32,7168]{2,1,0:T(8,128)(2,1)S(1)} %get-tuple-element.15), kind=kLoop, calls=%fused_computation.16 | loop fusion | flops 3440640 | bytes 3440640 | tf_op jit(solution)/shard_map/concatenate | solution.py:352
  (1 shorter events, 0.0 us)
Async XLA Ops:
  66.6 3.9 %copy-start.1 = (bf16[3,256,512]{2,1,0:T(8,128)(2,1)S(1)}, bf16[3,256,512]{2,1,0:T(8,128)(2,1)}, u32[]{:S(2)}) copy-start(bf16[3,256,512]{2,1,0:T(8,128)(2,1)} %get-tuple-element.14) | copy-start | bytes 2359300
  66.6 22.6 %collective-permute-start = (bf16[2,32,7168]{2,1,0:T(8,128)(2,1)}, bf16[2,32,7168]{2,1,0:T(8,128)(2,1)S(1)}, u32[]{:S(2)}, u32[]{:S(2)}) collective-permute-start(bf16[2,32,7168]{2,1,0:T(8,128)(2,1)} %bitcast.41), channel_id=1, source_target_pairs={{0,2},{1,3},{2,0},{3,1},{4,6},{5,7},{6,4},{7,5},{8,10},{9,11},{10,... | collective-permute-start | bytes 2752520 | tf_op jit(solution)/shard_map/ppermute | solution.py:343
  68.7 9.3 %slice-start = ((s8[7340032]{0:T(1024)(128)(4,1)}), s8[4194304]{0:T(1024)(128)(4,1)S(1)}, s32[]{:S(2)}) async-start(s8[7340032]{0:T(1024)(128)(4,1)} %bitcast.37), calls=%async_computation | async-start | bytes 8388608
  70.6 7.4 %slice-start.1 = ((s8[7340032]{0:T(1024)(128)(4,1)}), s8[3145728]{0:T(1024)(128)(4,1)S(1)}, s32[]{:S(2)}) async-start(s8[7340032]{0:T(1024)(128)(4,1)} %bitcast.37), calls=%async_computation.1 | async-start | bytes 6291456
  83.1 6.2 %copy-start = (bf16[2,2,32,7168]{3,2,1,0:T(8,128)(2,1)S(1)}, bf16[2,2,32,7168]{3,2,1,0:T(8,128)(2,1)}, u32[]{:S(2)}) copy-start(bf16[2,2,32,7168]{3,2,1,0:T(8,128)(2,1)} %get-tuple-element.10) | copy-start | bytes 5505028
